TPU v7x, 32 devices: a whole 2x2x4 slice. The times are simulated.
32 devices in a mesh: axial: 8 (over z, y), sector: 4 (over x, core).
Axes of the slice: x: 2, y: 2, z: 4, core: 2. Of those that a mesh axis runs over, the one named last changes fastest.
Arguments:
- start_field: float32 [5, 128, 32, 128], P(None, 'axial', 'sector'), may hold values from -6 to 6
- rhs: float32 [5, 128, 32, 128], P(None, 'axial', 'sector')
- dinv: float32 [5, 5, 128, 32, 128], P(None, None, 'axial', 'sector')
- lower: float32 [5, 5, 128, 32, 128], P(None, None, 'axial', 'sector')
- upper: float32 [5, 5, 128, 32, 128], P(None, None, 'axial', 'sector')
- az_left: float32 [5, 128, 32, 128], P(None, 'axial', 'sector')
- az_right: float32 [5, 128, 32, 128], P(None, 'axial', 'sector')
- counts: int32 [8, 4, 4], P('axial', 'sector'), may hold values from 32 to 128, as said below
- receiver_cells: int32 [8, 4, 4, 128], P('axial', 'sector'), may hold values from 0 to 16383
- donor_cell: int32 [8, 4, 4, 128], P('axial', 'sector'), may hold values from 0 to 16383
- iface_weight: float32 [8, 4, 5, 4, 128], P('axial', 'sector'), may hold values from -0.25 to 0.25
Outputs:
- adjoint_field: float32 [5, 128, 32, 128], P(None, 'axial', 'sector')
Inputs may be any that keep to these rules, and one draw needn't show every extreme that they name: Only the first counts[a, s, t] slots of each (a, s, t) are live; in every segment some sector receives 128 live slots from every sector.
All inputs are finite; a program needn't handle non-finite values.
Results may differ from a plain program's by a relative error of at most 0.0001.
Values sent between devices are 32-bit elements; how exact they have to be, the bound alone decides.
A program may use at most 128 MiB of HBM per device.

v0:
```python
import jax
import jax.numpy as jnp
from jax import lax
from jax.sharding import PartitionSpec as P

SWEEPS = 2


def padded_2(value, sides, width):
    for axis, dim in sides:
        size, length = (lax.axis_size(axis), value.shape[dim])
        up = [(i, (i + 1) % size) for i in range(size)]
        down = [(j, i) for i, j in up]
        last = lax.slice_in_dim(value, length - width, length, axis=dim)
        initial = lax.slice_in_dim(value, 0, width, axis=dim)
        before = lax.ppermute(last, axis, up)
        after = lax.ppermute(initial, axis, down)
        value = jnp.concatenate([before, value, after], axis=dim)
    return value


def shifted(value, axis, steps):
    count = lax.axis_size(axis)
    initial, last = (max(0, -steps), min(count, count - steps))
    return lax.ppermute(value, axis, [(source, source + steps) for source in range(initial, last)])


def apply_block(matrix, vector):
    return jnp.sum(matrix * vector[None], axis=1)


def compose(left_mat, trailing_operator):
    return jnp.sum(left_mat[:, :, None] * trailing_operator[None], axis=1)


def cycle_term(field_now, az_left, az_right):
    padded = padded_2(field_now, (("sector", 2),), 1)
    return az_left * padded[:, :, :-2] + az_right * padded[:, :, 2:]


def edge_plane(plane_now, offset_by):
    return shifted(plane_now, "axial", offset_by)


def sliding_boundary_contribution(field_now, counts, receiver_cells, donor_cell, iface_weight):
    fields = field_now.shape[0]
    flattened = field_now.reshape(fields, -1)
    cell_count = flattened.shape[1]
    receivers = receiver_cells.reshape(receiver_cells.shape[2], receiver_cells.shape[3])
    weights = iface_weight.reshape(fields, receivers.shape[0], receivers.shape[1])
    occupied = lax.broadcasted_iota(jnp.int32, receivers.shape, 1) < counts.reshape(-1, 1)
    picked = flattened[:, receivers]
    outgoing = jnp.where(occupied[None], weights * picked, 0.0)
    incoming = lax.all_to_all(outgoing, "sector", split_axis=1, concat_axis=1, tiled=True)
    donor_row_list = donor_cell.reshape(-1)
    gathered_sum = (
        jnp.zeros((fields, cell_count), jnp.float32)
        .at[:, donor_row_list]
        .add(incoming.reshape(fields, -1))
    )
    return gathered_sum.reshape(field_now.shape)


def carry_in(span_map, offset, zero_vec, reverse):
    all_maps, all_offsets = (
        lax.all_gather(span_map[None], "axial", axis=0, tiled=True),
        lax.all_gather(offset[None], "axial", axis=0, tiled=True),
    )
    group_elements = all_maps.shape[0]
    position = lax.axis_index("axial")

    def absorb(j, carried):
        member_id = group_elements - 1 - j if reverse else j
        earlier = member_id > position if reverse else member_id < position
        matrix = lax.dynamic_index_in_dim(all_maps, member_id, 0, False)
        pushed = lax.dynamic_index_in_dim(all_offsets, member_id, 0, False)
        return jnp.where(earlier, apply_block(matrix, carried) + pushed, carried)

    return lax.fori_loop(0, group_elements, absorb, zero_vec)


def unit_shapes(matrices):
    fields = matrices.shape[0]
    line_shape = matrices.shape[3:]
    identity_map = jnp.broadcast_to(
        jnp.eye(fields, dtype=jnp.float32)[:, :, None, None], (fields, fields) + line_shape
    )
    zero_vec = jnp.zeros((fields,) + line_shape, jnp.float32)
    return (identity_map, zero_vec)


def plane_index(i, planes, reverse):
    return planes - 1 - i if reverse else i


def local_sweep(matrices, drive, reverse):
    planes = drive.shape[1]
    identity_map, zero_vec = unit_shapes(matrices)

    def plane_at(i):
        plane_id = plane_index(i, planes, reverse)
        matrix = lax.dynamic_index_in_dim(matrices, plane_id, 2, False)
        pushed = lax.dynamic_index_in_dim(drive, plane_id, 1, False)
        return (plane_id, matrix, pushed)

    def compose_step(i, carried):
        plane_id, matrix, pushed = plane_at(i)
        return (compose(matrix, carried[0]), apply_block(matrix, carried[1]) + pushed)

    span_map, offset = lax.fori_loop(0, planes, compose_step, (identity_map, zero_vec))
    entry = carry_in(span_map, offset, zero_vec, reverse)

    def replay(i, carried):
        plane_id, matrix, pushed = plane_at(i)
        updated = apply_block(matrix, carried[0]) + pushed
        return (updated, lax.dynamic_update_index_in_dim(carried[1], updated, plane_id, 1))

    return lax.fori_loop(0, planes, replay, (entry, jnp.zeros_like(drive)))[1]


def shards(
    start_field,
    rhs,
    dinv,
    lower,
    upper,
    az_left,
    az_right,
    counts,
    receiver_cells,
    donor_cell,
    iface_weight,
):
    low_steps = -compose(dinv, lower)
    high_steps = -compose(dinv, upper)
    field_now = start_field
    for sweep_id in range(SWEEPS):
        next_edge = edge_plane(field_now[:, :1], -1)
        next_planes = jnp.concatenate([field_now[:, 1:], next_edge], axis=1)
        forcing_vector = (
            rhs
            + cycle_term(field_now, az_left, az_right)
            + sliding_boundary_contribution(
                field_now, counts, receiver_cells, donor_cell, iface_weight
            )
            - apply_block(upper, next_planes)
        )
        field_now = local_sweep(low_steps, apply_block(dinv, forcing_vector), False)
        prev_edge = edge_plane(field_now[:, -1:], 1)
        behind = jnp.concatenate([prev_edge, field_now[:, :-1]], axis=1)
        forcing_vector = (
            rhs
            + cycle_term(field_now, az_left, az_right)
            + sliding_boundary_contribution(
                field_now, counts, receiver_cells, donor_cell, iface_weight
            )
            - apply_block(lower, behind)
        )
        field_now = local_sweep(high_steps, apply_block(dinv, forcing_vector), True)
    return field_now


def solution(mesh):
    in_specs = (
        P(None, "axial", "sector", None),
        P(None, "axial", "sector", None),
        P(None, None, "axial", "sector", None),
        P(None, None, "axial", "sector", None),
        P(None, None, "axial", "sector", None),
        P(None, "axial", "sector", None),
        P(None, "axial", "sector", None),
        P("axial", "sector", None),
        P("axial", "sector", None, None),
        P("axial", "sector", None, None),
        P("axial", "sector", None, None, None),
    )
    out_specs = P(None, "axial", "sector", None)
    return jax.shard_map(shards, mesh=mesh, in_specs=in_specs, out_specs=out_specs, check_vma=False)
```

profile of v0, /device:TPU:0, one launch (start us, length us, event | category | flops | bytes accessed | tf_op | source)
XLA Modules:
  0.0 675.9 jit_solution(1694392318219126991)
XLA Ops:
  0.7 6.0 copy.59
  6.8 4.4 gather_fusion
  14.0 4.2 all-to-all-start
  24.6 4.6 multiply_reduce_fusion.8
  30.6 1.6 neg.7
  34.6 1.6 neg.6
  39.6 6.3 scatter_custom_fusion
  46.0 5.9 copy.62
  55.4 27.8 %while.196 = (s32[]{:T(128)}, f32[5,5,8,128]{3,2,1,0:T(8,128)S(1)}, f32[5,8,128]{2,1,0:T(8,128)S(1)}, f32[5,5,16,8,128]{4,3,1,0,2:T(8,128)}, f32[5,16,8,128]{3,2,1,0:T(8,128)}, /*index=5*/s32[]{:T(128)}, s32[]{:T(128)}) while((s32[]{:T(128)}, f32[5,5,8,128]{3,2,1,0:T(8,128)S(1)}, f32[5,8,128]{2,1,0:T(8,128)S(1)}, ...), condition=%wide.region_8.9_spmd.clone, body=%wide.region_5.8_spmd.clone.sunk | while | flops 286723 | bytes 860255 | solution.py:110
  83.2 37.0 %all-gather = f32[40,5,8,128]{3,2,1,0:T(8,128)} all-gather(f32[5,5,8,128]{3,2,1,0:T(8,128)S(1)} %get-tuple-element.1365), channel_id=2, replica_groups=mesh['axial'=8,'sector'=4] {'axial'}, dimensions={0}, use_global_device_ids=true | all-gather | bytes 921600 | tf_op jit(solution)/shard_map/all_gather | solution.py:66
  120.3 32.6 %all-gather.1 = f32[40,8,128]{2,1,0:T(8,128)} all-gather(f32[5,8,128]{2,1,0:T(8,128)S(1)} %get-tuple-element.1366), channel_id=3, replica_groups=mesh['axial'=8,'sector'=4] {'axial'}, dimensions={0}, use_global_device_ids=true | all-gather | bytes 184320 | tf_op jit(solution)/shard_map/all_gather | solution.py:67
  152.9 13.3 %while.197 = (s32[]{:T(128)}, f32[5,8,128]{2,1,0:T(8,128)S(1)}, s32[]{:T(128)}, f32[8,5,5,8,128]{4,3,2,1,0:T(8,128)}, f32[8,5,8,128]{3,2,1,0:T(8,128)}, /*index=5*/s32[]{:T(128)}, s32[]{:T(128)}) while((s32[]{:T(128)}, f32[5,8,128]{2,1,0:T(8,128)S(1)}, s32[]{:T(128)}, f32[8,5,5,8,128]{4,3,2,1,0:T(8,128)}, ...), condition=%wide.region_11.12_spmd.clone, body=%wide.region_9.11_spmd.clone.sunk | while | flops 66564 | bytes 266346 | solution.py:79
  166.9 47.8 %while.192 = (s32[]{:T(128)}, f32[5,8,128]{2,1,0:T(8,128)S(1)}, f32[5,16,8,128]{3,2,1,0:T(8,128)}, f32[5,5,16,8,128]{4,3,2,1,0:T(8,128)}, f32[5,16,8,128]{3,2,1,0:T(8,128)}, /*index=5*/s32[]{:T(128)}) while((s32[]{:T(128)}, f32[5,8,128]{2,1,0:T(8,128)S(1)}, f32[5,16,8,128]{3,2,1,0:T(8,128)}, f32[5,5,16,8,128]{4,3,2,1,0:T(8,128)}, ...), condition=%wide.region_14.15_spmd, body=%wide.region_12.14_spmd.sunk | while | flops 56322 | bytes 266829 | solution.py:118
  167.8 1.4 fusion.75
  179.8 1.3 fusion.75
  182.8 1.4 fusion.75
  185.8 1.4 fusion.75
  188.8 1.4 fusion.75
  194.7 1.3 fusion.75
  200.7 1.3 fusion.75
  206.7 1.3 fusion.75
  209.7 1.3 fusion.75
  215.5 5.9 copy.64
  221.4 3.3 collective-permute-start.5
  224.7 5.0 gather_fusion.1
  231.4 3.3 all-to-all-start.1
  235.8 1.7 slice.91
  240.1 6.3 scatter_custom_fusion.1
  246.4 5.9 copy.67
  253.5 1.6 multiply_reduce_fusion.15
  257.2 28.0 %while.198 = (s32[]{:T(128)}, f32[5,5,8,128]{3,2,1,0:T(8,128)S(1)}, f32[5,8,128]{2,1,0:T(8,128)S(1)}, f32[5,5,16,8,128]{4,3,1,0,2:T(8,128)}, f32[5,16,8,128]{3,2...) while((s32[]{:T(128)}, f32[5,5,8,128]{3,2,1,0:T(8,128)S(1)}, ...), condition=%wide.region_21.22_spmd.clone, body=%wide.region_18.21_spmd.clone.sunk | while | flops 286727 | bytes 860317 | solution.py:110
  285.2 34.3 %all-gather.2 = f32[40,5,8,128]{3,2,1,0:T(8,128)} all-gather(f32[5,5,8,128]{3,2,1,0:T(8,128)S(1)} %get-tuple-element.1369), channel_id=4, replica_groups=mesh['axial'=8,'sector'=4] {'axial'}, dimensions={0}, use_global_device_ids=true | all-gather | bytes 921600 | tf_op jit(solution)/shard_map/all_gather | solution.py:66
  319.5 32.6 %all-gather.3 = f32[40,8,128]{2,1,0:T(8,128)} all-gather(f32[5,8,128]{2,1,0:T(8,128)S(1)} %get-tuple-element.1370), channel_id=5, replica_groups=mesh['axial'=8,'sector'=4] {'axial'}, dimensions={0}, use_global_device_ids=true | all-gather | bytes 184320 | tf_op jit(solution)/shard_map/all_gather | solution.py:67
  352.1 13.3 %while.199 = (s32[]{:T(128)}, f32[5,8,128]{2,1,0:T(8,128)S(1)}, s32[]{:T(128)}, f32[8,5,5,8,128]{4,3,2,1,0:T(8,128)}, f32[8,5,8,128]{3,2,1,0:T(8,128)}, /*index=5*/s32[]{:T(128)}, s32[]{:T(128)}, s32[]{:T(128)}, s32[]{:T(128)}) while((s32[]{:T(128)}, f32[5,8,128]{2,1,0:T(8,128)S(1)}, s32[]{:T(128)}, ...), condition=%wide.region_24.25_spmd.clone, body=%wide.region_22.24_spmd.clone.sunk | while | flops 66568 | bytes 266408 | solution.py:79
  366.2 47.8 %while.193 = (s32[]{:T(128)}, f32[5,8,128]{2,1,0:T(8,128)S(1)}, f32[5,16,8,128]{3,2,1,0:T(8,128)}, f32[5,5,16,8,128]{4,3,2,1,0:T(8,128)}, f32[5,16,8,128]{3,2,1,...) while((s32[]{:T(128)}, f32[5,8,128]{2,1,0:T(8,128)S(1)}, f32[5,16,8,128]{3,2,1,0:T(8,128)}, ...), condition=%wide.region_27.28_spmd, body=%wide.region_25.27_spmd.sunk | while | flops 56326 | bytes 266391 | solution.py:118
  370.1 1.3 fusion.77
  379.1 1.3 fusion.77
  385.0 1.3 fusion.77
  391.0 1.4 fusion.77
  394.0 1.4 fusion.77
  397.0 1.4 fusion.77
  400.0 1.3 fusion.77
  412.0 1.4 fusion.77
  414.0 5.9 copy.69
  420.7 5.0 gather_fusion.2
  427.4 3.3 all-to-all-start.2
  433.1 1.7 slice.96
  437.4 6.3 scatter_custom_fusion.2
  443.7 5.9 copy.72
  452.4 16.4 %while.200 = (s32[]{:T(128)}, f32[5,5,8,128]{3,2,1,0:T(8,128)S(1)}, f32[5,8,128]{2,1,0:T(8,128)S(1)}, f32[5,5,16,8,128]{4,3,1,0,2:T(8,128)}, f32[5,16,8,128]{3,2,1,0:T(8,128)S(1)}, /*index=5*/s32[]{:T(128)}, s32[]{:T(128)}) while((s32[]{:T(128)}, f32[5,5,8,128]{3,2,1,0:T(8,128)S(1)}, f32[5,8,128]{2,1,0:T(8,128)S(1)}, ...), condition=%wide.region_34.35_spmd.clone, body=%wide.region_31.34_spmd.clone.sunk | while | flops 286723 | bytes 860255 | solution.py:110
  468.8 32.3 %all-gather.4 = f32[40,5,8,128]{3,2,1,0:T(8,128)S(1)} all-gather(f32[5,5,8,128]{3,2,1,0:T(8,128)S(1)} %get-tuple-element.1373), channel_id=6, replica_groups=mesh['axial'=8,'sector'=4] {'axial'}, dimensions={0}, use_global_device_ids=true | all-gather | bytes 921600 | tf_op jit(solution)/shard_map/all_gather | solution.py:66
  501.1 30.7 %all-gather.5 = f32[40,8,128]{2,1,0:T(8,128)S(1)} all-gather(f32[5,8,128]{2,1,0:T(8,128)S(1)} %get-tuple-element.1374), channel_id=7, replica_groups=mesh['axial'=8,'sector'=4] {'axial'}, dimensions={0}, use_global_device_ids=true | all-gather | bytes 184320 | tf_op jit(solution)/shard_map/all_gather | solution.py:67
  532.4 15.5 %while.194 = (s32[]{:T(128)}, f32[5,8,128]{2,1,0:T(8,128)S(1)}, f32[5,16,8,128]{3,2,1,0:T(8,128)S(1)}, f32[5,5,16,8,128]{4,3,2,1,0:T(8,128)}, f32[5,16,8,128]{3,2,1,0:T(8,128)S(1)}, /*index=5*/s32[]{:T(128)}) while((s32[]{:T(128)}, f32[5,8,128]{2,1,0:T(8,128)S(1)}, f32[5,16,8,128]{3,2,1,0:T(8,128)S(1)}, f32[5,5,16,8,128]{4,3,2,1,0:T(8,128)}, ...), condition=%wide.region_40.41_spmd, body=%wide.region_38.40_spmd.sunk | while | flops 56322 | bytes 266321 | solution.py:118
  548.0 4.7 copy.74
  552.7 4.4 gather_fusion.3
  557.9 3.3 all-to-all-start.3
  561.1 1.6 collective-permute-start.11
  563.6 1.5 collective-permute-start.10
  565.3 6.1 scatter_custom_fusion.3
  571.3 6.0 copy.77
  579.3 16.5 %while.202 = (s32[]{:T(128)}, f32[5,5,8,128]{3,2,1,0:T(8,128)S(1)}, f32[5,8,128]{2,1,0:T(8,128)S(1)}, f32[5,5,16,8,128]{4,3,1,0,2:T(8,128)}, f32[5,16,8,128]{3,2...) while((s32[]{:T(128)}, f32[5,5,8,128]{3,2,1,0:T(8,128)S(1)}, ...), condition=%wide.region_47.48_spmd.clone, body=%wide.region_44.47_spmd.clone.sunk | while | flops 286727 | bytes 860317 | solution.py:110
  595.9 32.3 %all-gather.6 = f32[40,5,8,128]{3,2,1,0:T(8,128)S(1)} all-gather(f32[5,5,8,128]{3,2,1,0:T(8,128)S(1)} %get-tuple-element.1377), channel_id=8, replica_groups=mesh['axial'=8,'sector'=4] {'axial'}, dimensions={0}, use_global_device_ids=true | all-gather | bytes 921600 | tf_op jit(solution)/shard_map/all_gather | solution.py:66
  628.2 30.6 %all-gather.7 = f32[40,8,128]{2,1,0:T(8,128)S(1)} all-gather(f32[5,8,128]{2,1,0:T(8,128)S(1)} %get-tuple-element.1378), channel_id=9, replica_groups=mesh['axial'=8,'sector'=4] {'axial'}, dimensions={0}, use_global_device_ids=true | all-gather | bytes 184320 | tf_op jit(solution)/shard_map/all_gather | solution.py:67
  659.5 15.6 %while.195 = (s32[]{:T(128)}, f32[5,8,128]{2,1,0:T(8,128)S(1)}, f32[5,16,8,128]{3,2,1,0:T(8,128)S(1)}, f32[5,5,16,8,128]{4,3,2,1,0:T(8,128)}, f32[5,16,8,128]{3,...) while((s32[]{:T(128)}, f32[5,8,128]{2,1,0:T(8,128)S(1)}, ...), condition=%wide.region_53.54_spmd, body=%wide.region_51.53_spmd.sunk | while | flops 56326 | bytes 266391 | solution.py:118
  (756 shorter events, 262.5 us)
Async XLA Ops:
  0.7 6.1 copy-start.31
  0.7 11.9 %copy-start.28 = (f32[1,1,5,4,128]{4,3,2,1,0:T(4,128)S(1)}, f32[1,1,5,4,128]{4,3,2,1,0:T(4,128)}, u32[]{:S(2)}) copy-start(f32[1,1,5,4,128]{4,3,2,1,0:T(4,128)} %param.45) | copy-start | bytes 30724
  0.7 23.8 %copy-start = (f32[5,5,16,8,128]{4,3,2,1,0:T(8,128)S(1)}, f32[5,5,16,8,128]{4,3,2,1,0:T(8,128)}, u32[]{:S(2)}) copy-start(f32[5,5,16,8,128]{4,3,2,1,0:T(8,128)} %param.37) | copy-start | bytes 4915204
  0.7 23.8 %copy-start.1 = (f32[5,5,16,8,128]{4,3,2,1,0:T(8,128)S(1)}, f32[5,5,16,8,128]{4,3,2,1,0:T(8,128)}, u32[]{:S(2)}) copy-start(f32[5,5,16,8,128]{4,3,2,1,0:T(8,128)} %param.39) | copy-start | bytes 4915204
  12.6 1.3 copy-start.34
  14.0 24.8 %all-to-all-start = ((f32[5,4,128]{2,0,1:T(8,128)}), f32[5,4,128]{2,0,1:T(8,128)S(1)}, u32[]{:S(2)}, u32[]{:S(2)}) async-start(f32[5,4,128]{2,0,1:T(8,128)} %fusion.51), calls=%async_computation | async-start | bytes 32768 | tf_op jit(solution)/shard_map/all_to_all | solution.py:54
  19.3 33.9 %collective-permute-start = (f32[5,16,1,128]{3,2,1,0:T(1,128)S(1)}, f32[5,16,1,128]{3,2,1,0:T(1,128)}, u32[]{:S(2)}, u32[]{:S(2)}) collective-permute-start(f32[5,16,1,128]{3,2,1,0:T(1,128)S(1)} %get-tuple-element.1681), channel_id=1, source_target_pairs={{0,1},{1,2},{2,3},{3,0},{4,5},{5,6},{6,7},{7,4},{8,9},{9,10},{10,1... | collective-permute-start | bytes 122888 | tf_op jit(solution)/shard_map/ppermute | solution.py:16
  19.9 33.4 %collective-permute-start.1 = (f32[5,16,1,128]{3,2,1,0:T(1,128)S(1)}, f32[5,16,1,128]{3,2,1,0:T(1,128)}, u32[]{:S(2)}, u32[]{:S(2)}) collective-permute-start(f32[5,16,1,128]{3,2,1,0:T(1,128)S(1)} %get-tuple-element.1682), channel_id=1, source_target_pairs={{1,0},{2,1},{3,2},{0,3},{5,4},{6,5},{7,6},{4,7},{9,8},{10,9},{11,1... | collective-permute-start | bytes 122888 | tf_op jit(solution)/shard_map/ppermute | solution.py:17
  22.5 29.4 %collective-permute-start.2 = (f32[5,1,8,128]{3,2,1,0:T(8,128)}, f32[5,1,8,128]{3,2,1,0:T(8,128)}, u32[]{:S(2)}, u32[]{:S(2)}) collective-permute-start(f32[5,1,8,128]{3,2,1,0:T(8,128)} %slice.85), channel_id=1, source_target_pairs={{4,0},{8,4},{12,8},{16,12},{20,16},{24,20},{28,24},{5,1},{9,5},{13... | collective-permute-start | bytes 61448 | tf_op jit(solution)/shard_map/ppermute | solution.py:25
  24.5 15.1 %copy-start.38 = (s32[512,1]{0,1:T(1,128)}, s32[512,1]{0,1:T(1,128)S(1)}, u32[]{:S(2)}) copy-start(s32[512,1]{0,1:T(1,128)S(1)} %compare_select_fusion) | copy-start | bytes 6148
  24.5 5.2 copy-start.21
  32.1 1.2 copy-start.4
  36.2 1.3 copy-start.3
  51.9 1.4 copy-start.9
  51.9 1.4 copy-start.13
  51.9 1.4 copy-start.17
  51.9 1.4 copy-start.22
  51.9 1.5 copy-start.26
  54.4 0.9 copy-start.29
  215.5 9.2 %copy-start.32 = (s32[1024]{0:T(1024)S(1)}, s32[1024]{0:T(1024)}, u32[]{:S(2)}) copy-start(s32[1024]{0:T(1024)} %copy-done.31) | copy-start | bytes 12292
  215.5 15.3 %copy-start.35 = (pred[4,128]{1,0:T(4,128)(4,1)S(1)}, pred[4,128]{1,0:T(4,128)(4,1)}, u32[]{:S(2)}) copy-start(pred[4,128]{1,0:T(4,128)(4,1)} %copy-done.34) | copy-start | bytes 1540
  221.4 31.0 %collective-permute-start.5 = (f32[5,1,8,128]{3,2,1,0:T(8,128)S(1)}, f32[5,1,8,128]{3,2,1,0:T(8,128)S(1)}, u32[]{:S(2)}, u32[]{:S(2)}) collective-permute-start(f32[5,1,8,128]{3,2,1,0:T(8,128)S(1)} %slice.90), channel_id=1, source_target_pairs={{0,4},{4,8},{8,12},{12,16},{16,20},{20,24},{24,28},{1,5},{5,9},{9,... | collective-permute-start | bytes 61448 | tf_op jit(solution)/shard_map/ppermute | solution.py:25
  231.4 7.9 %all-to-all-start.1 = ((f32[5,4,128]{2,0,1:T(8,128)}), f32[5,4,128]{2,0,1:T(8,128)S(1)}, u32[]{:S(2)}, u32[]{:S(2)}) async-start(f32[5,4,128]{2,0,1:T(8,128)} %fusion.50), calls=%async_computation.1 | async-start | bytes 32768 | tf_op jit(solution)/shard_map/all_to_all | solution.py:54
  237.5 17.7 %collective-permute-start.3 = (f32[5,16,1,128]{3,2,1,0:T(1,128)S(1)}, f32[5,16,1,128]{3,2,1,0:T(1,128)}, u32[]{:S(2)}, u32[]{:S(2)}) collective-permute-start(f32[5,16,1,128]{3,2,1,0:T(1,128)S(1)} %get-tuple-element.1679), channel_id=1, source_target_pairs={{0,1},{1,2},{2,3},{3,0},{4,5},{5,6},{6,7},{7,4},{8,9},{9,10},{10,1... | collective-permute-start | bytes 122888 | tf_op jit(solution)/shard_map/ppermute | solution.py:16
  238.0 17.2 %collective-permute-start.4 = (f32[5,16,1,128]{3,2,1,0:T(1,128)S(1)}, f32[5,16,1,128]{3,2,1,0:T(1,128)}, u32[]{:S(2)}, u32[]{:S(2)}) collective-permute-start(f32[5,16,1,128]{3,2,1,0:T(1,128)S(1)} %get-tuple-element.1680), channel_id=1, source_target_pairs={{1,0},{2,1},{3,2},{0,3},{5,4},{6,5},{7,6},{4,7},{9,8},{10,9},{11,1... | collective-permute-start | bytes 122888 | tf_op jit(solution)/shard_map/ppermute | solution.py:17
  252.4 2.8 copy-start.5
  252.4 2.8 copy-start.10
  252.4 2.8 copy-start.14
  252.4 2.8 copy-start.18
  252.4 2.8 copy-start.23
  256.2 0.9 copy-start.30
  414.0 12.7 %copy-start.36 = (pred[4,128]{1,0:T(4,128)(4,1)S(1)}, pred[4,128]{1,0:T(4,128)(4,1)}, u32[]{:S(2)}) copy-start(pred[4,128]{1,0:T(4,128)(4,1)} %copy-done.34) | copy-start | bytes 1540
  427.4 9.2 %all-to-all-start.2 = ((f32[5,4,128]{2,0,1:T(8,128)}), f32[5,4,128]{2,0,1:T(8,128)S(1)}, u32[]{:S(2)}, u32[]{:S(2)}) async-start(f32[5,4,128]{2,0,1:T(8,128)} %fusion.49), calls=%async_computation.2 | async-start | bytes 32768 | tf_op jit(solution)/shard_map/all_to_all | solution.py:54
  430.6 19.1 %collective-permute-start.8 = (f32[5,1,8,128]{3,2,1,0:T(8,128)S(1)}, f32[5,1,8,128]{3,2,1,0:T(8,128)S(1)}, u32[]{:S(2)}, u32[]{:S(2)}) collective-permute-start(f32[5,1,8,128]{3,2,1,0:T(8,128)S(1)} %slice.97), channel_id=1, source_target_pairs={{4,0},{8,4},{12,8},{16,12},{20,16},{24,20},{28,24},{5,1},{9,5},{13... | collective-permute-start | bytes 61448 | tf_op jit(solution)/shard_map/ppermute | solution.py:25
  434.8 16.2 %collective-permute-start.6 = (f32[5,16,1,128]{3,2,1,0:T(1,128)S(1)}, f32[5,16,1,128]{3,2,1,0:T(1,128)S(1)}, u32[]{:S(2)}, u32[]{:S(2)}) collective-permute-start(f32[5,16,1,128]{3,2,1,0:T(1,128)S(1)} %get-tuple-element.1677), channel_id=1, source_target_pairs={{0,1},{1,2},{2,3},{3,0},{4,5},{5,6},{6,7},{7,4},{8,9},{9,10},{10,1... | collective-permute-start | bytes 122888 | tf_op jit(solution)/shard_map/ppermute | solution.py:16
  435.2 15.8 %collective-permute-start.7 = (f32[5,16,1,128]{3,2,1,0:T(1,128)S(1)}, f32[5,16,1,128]{3,2,1,0:T(1,128)}, u32[]{:S(2)}, u32[]{:S(2)}) collective-permute-start(f32[5,16,1,128]{3,2,1,0:T(1,128)S(1)} %get-tuple-element.1678), channel_id=1, source_target_pairs={{1,0},{2,1},{3,2},{0,3},{5,4},{6,5},{7,6},{4,7},{9,8},{10,9},{11,1... | collective-permute-start | bytes 122888 | tf_op jit(solution)/shard_map/ppermute | solution.py:17
  449.7 1.3 copy-start.6
  449.7 1.4 copy-start.11
  449.7 1.4 copy-start.15
  449.7 1.4 copy-start.19
  449.7 1.4 copy-start.24
  548.0 14.9 %copy-start.7 = (f32[5,16,8,128]{3,2,1,0:T(8,128)}, f32[5,16,8,128]{3,2,1,0:T(8,128)S(1)}, u32[]{:S(2)}) copy-start(f32[5,16,8,128]{3,2,1,0:T(8,128)S(1)} %get-tuple-element.1376) | copy-start | bytes 983044
  548.0 4.7 copy-start.33
  548.0 9.3 %copy-start.37 = (pred[4,128]{1,0:T(4,128)(4,1)S(1)}, pred[4,128]{1,0:T(4,128)(4,1)}, u32[]{:S(2)}) copy-start(pred[4,128]{1,0:T(4,128)(4,1)} %copy-done.34) | copy-start | bytes 1540
  557.9 7.2 %all-to-all-start.3 = ((f32[5,4,128]{2,0,1:T(8,128)}), f32[5,4,128]{2,0,1:T(8,128)S(1)}, u32[]{:S(2)}, u32[]{:S(2)}) async-start(f32[5,4,128]{2,0,1:T(8,128)} %fusion.48), calls=%async_computation.3 | async-start | bytes 32768 | tf_op jit(solution)/shard_map/all_to_all | solution.py:54
  561.1 16.3 %collective-permute-start.11 = (f32[5,1,8,128]{3,2,1,0:T(8,128)S(1)}, f32[5,1,8,128]{3,2,1,0:T(8,128)S(1)}, u32[]{:S(2)}, u32[]{:S(2)}) collective-permute-start(f32[5,1,8,128]{3,2,1,0:T(8,128)S(1)} %slice.102), channel_id=1, source_target_pairs={{0,4},{4,8},{8,12},{12,16},{16,20},{20,24},{24,28},{1,5},{5,9},{9,... | collective-permute-start | bytes 61448 | tf_op jit(solution)/shard_map/ppermute | solution.py:25
  563.6 15.1 %collective-permute-start.10 = (f32[5,16,1,128]{3,2,1,0:T(1,128)S(1)}, f32[5,16,1,128]{3,2,1,0:T(1,128)S(1)}, u32[]{:S(2)}, u32[]{:S(2)}) collective-permute-start(f32[5,16,1,128]{3,2,1,0:T(1,128)S(1)} %get-tuple-element.1676), channel_id=1, source_target_pairs={{1,0},{2,1},{3,2},{0,3},{5,4},{6,5},{7,6},{4,7},{9,8},{10,9},{11,1... | collective-permute-start | bytes 122888 | tf_op jit(solution)/shard_map/ppermute | solution.py:17
  565.1 13.6 %collective-permute-start.9 = (f32[5,16,1,128]{3,2,1,0:T(1,128)S(1)}, f32[5,16,1,128]{3,2,1,0:T(1,128)S(1)}, u32[]{:S(2)}, u32[]{:S(2)}) collective-permute-start(f32[5,16,1,128]{3,2,1,0:T(1,128)S(1)} %get-tuple-element.1675), channel_id=1, source_target_pairs={{0,1},{1,2},{2,3},{3,0},{4,5},{5,6},{6,7},{7,4},{8,9},{9,10},{10,1... | collective-permute-start | bytes 122888 | tf_op jit(solution)/shard_map/ppermute | solution.py:16
  571.3 7.2 %copy-start.2 = (f32[5,5,16,8,128]{4,3,2,1,0:T(8,128)S(1)}, f32[5,5,16,8,128]{4,3,2,1,0:T(8,128)}, u32[]{:S(2)}) copy-start(f32[5,5,16,8,128]{4,3,2,1,0:T(8,128)} %param.38) | copy-start | bytes 4915204
  577.4 1.4 copy-start.8
  577.4 1.4 copy-start.12
  577.4 1.4 copy-start.16
  577.4 1.4 copy-start.20
  577.4 1.4 copy-start.25
  675.1 0.7 copy-start.27
where the time goes:
time: 689 us; the launch traced here: 676 us
  other arithmetic  289 us (42%)
  blocking collectives  262 us (38%)
  local copies, waits for them, and re-layouts  90.6 us (13%)
  starting transfers between devices  28.4 us (4%)
    all_gather x4, blocking collectives, carry_in(): lax.all_gather(span_map[None], 'axial', axis=0, tiled=True)  136 us
    reduce_sum x168, other arithmetic, apply_block(): return jnp.sum(matrix * vector[None], axis=1)  136 us
    all_gather x4, blocking collectives, carry_in(): lax.all_gather(offset[None], 'axial', axis=0, tiled=True)  126 us
    dynamic_update_slice x64, other arithmetic, replay(): lax.dynamic_update_index_in_dim(carried[1], updated, plane_id, 1)  43.5 us
    scatter-add x4, other arithmetic, sliding_boundary_contribution(): gathered_sum = jnp.zeros((fields, cell_count), jnp.float32).at[:, donor_r...  25.1 us
    add x64, other arithmetic, compose_step(): apply_block(matrix, carried[1]) + pushed  24.1 us
    add x64, other arithmetic, replay(): updated = apply_block(matrix, carried[0]) + pushed  23.8 us
    reshape x4, local copies, waits for them, and re-layouts, sliding_boundary_contribution(): return gathered_sum.reshape(field_now.shape)  23.8 us
  transfers between devices with their start and end apart: 16, of which 0 were waited for; matrix products, arithmetic and copies ran while one was open for 13% of the time, Pallas kernels for 0%

commit v1 on v0

v1 whole, which is shorter than its diff:
```python
import functools

import jax
import jax.numpy as jnp
from jax import lax
from jax.experimental import pallas as pl
from jax.experimental.pallas import tpu as pltpu
from jax.sharding import PartitionSpec as P

SWEEPS = 2
MESH = pl.DeviceIdType.MESH
BF = jnp.bfloat16
F32 = jnp.float32


def split(x):
    hi = x.astype(BF)
    return hi, (x - hi.astype(F32)).astype(BF)


def kernel(n_ax, n_sec, start, rhs, dinv, lower, upper, azl, azr, counts, recv_cells, donor, weight, out,
           fld, low_step, high_step, maps, map_in, offs, off_in, entry, edge, halo_out, halo_in,
           slot_out, slot_in, part, drive, pick_row, pick_lane, put_row, put_lane, live_w, iface,
           map_ss, map_rs, off_ss, off_rs, edge_ss, edge_rs, halo_ss, halo_rs, slot_ss, slot_rs):
    fields, planes, az, rad = rhs.shape
    cap = recv_cells.shape[-1]
    rows = planes * az
    fr = range(fields)
    a, s = lax.axis_index("axial"), lax.axis_index("sector")
    right, left = lax.rem(s + 1, n_sec), lax.rem(s + n_sec - 1, n_sec)
    halves = 2 * SWEEPS

    barrier = pltpu.get_barrier_semaphore()
    for e in range(1, n_sec):
        pl.semaphore_signal(barrier, inc=1, device_id={"sector": lax.rem(s + e, n_sec)}, device_id_type=MESH)
    for d in range(1, n_ax):
        pl.semaphore_signal(barrier, inc=1, device_id={"axial": lax.rem(a + d, n_ax)}, device_id_type=MESH)

    def place(direction):
        return (a, 1) if direction == 0 else (n_ax - 1 - a, -1)

    def remote(src, dst, ss, rs, **device):
        return pltpu.make_async_remote_copy(src_ref=src, dst_ref=dst, send_sem=ss, recv_sem=rs,
                                            device_id=device, device_id_type=MESH)

    def peer(direction, d):
        return lax.rem(a + place(direction)[1] * d + n_ax, n_ax)

    def map_copy(direction, d):
        return remote(maps.at[direction], map_in.at[direction, d], map_ss.at[direction, d],
                      map_rs.at[direction, d], axial=peer(direction, d))

    def off_copy(h, d):
        return remote(offs.at[h], off_in.at[h, d], off_ss.at[h, d], off_rs.at[h, d], axial=peer(h % 2, d))

    def map_range(direction):
        q, _ = place(direction)
        return 1, jnp.where(q >= 1, n_ax - q, 1)

    def edge_copy():
        return remote(start.at[:, 0], edge, edge_ss.at[0], edge_rs.at[0], axial=lax.rem(a + n_ax - 1, n_ax))

    def halo_copy(h, side):
        return remote(halo_out.at[h, side], halo_in.at[h, side], halo_ss.at[h, side], halo_rs.at[h, side],
                      sector=right if side == 0 else left)

    def slot_copy(h, e, sending):
        target = lax.rem(s + e, n_sec)
        owner = s if sending else lax.rem(s + n_sec - e, n_sec)
        return remote(slot_out.at[h, target], slot_in.at[h, owner], slot_ss.at[h, e], slot_rs.at[h, e],
                      sector=target)

    def each(low, high, body):
        def step(d, c):
            body(d)
            return c
        lax.fori_loop(low, high, step, 0)

    def one_hots(cells, row_ref, lane_ref):
        down = lax.broadcasted_iota(jnp.int32, (rows, cap), 0)
        across = lax.broadcasted_iota(jnp.int32, (rad, cap), 0)
        for t in range(n_sec):
            idx = cells[0, 0, pl.ds(t, 1), :]
            cols = slice(t * cap, (t + 1) * cap)
            row_ref[0:rows, cols] = jnp.where(down == idx // rad, 1.0, 0.0).astype(BF)
            lane_ref[:, cols] = jnp.where(across == lax.rem(idx, rad), 1.0, 0.0)

    def times(mat, p, x):
        return [sum(mat[i, j, p] * x[j] for j in fr) for i in fr]

    def send_field(h):
        for side, layer in ((0, az - 1), (1, 0)):
            halo_out[h, side] = fld[:, 1:planes + 1, layer, :]
        for side in range(2):
            halo_copy(h, side).start()
        for f in fr:
            turned = fld[f, 1:planes + 1].reshape(rows, rad).T
            hi, lo = split(turned)
            got = (jnp.dot(hi, pick_row[...], preferred_element_type=F32)
                   + jnp.dot(lo, pick_row[...], preferred_element_type=F32))
            line = jnp.sum(got * pick_lane[...], axis=0, keepdims=True) * live_w[pl.ds(f, 1), :]
            for t in range(n_sec):
                slot_out[h, t, pl.ds(f, 1), :] = line[:, t * cap:(t + 1) * cap]
        for e in range(1, n_sec):
            slot_copy(h, e, True).start()
        slot_in[h, s] = slot_out[h, s]

    def build_map(coupling, steps, direction):
        for i in fr:
            for j in fr:
                maps[direction, i, j] = jnp.full((az, rad), 1.0 if i == j else 0.0, F32)

        def step(i, c):
            p = i if direction == 0 else planes - 1 - i
            for col in fr:
                v = times(dinv, p, [coupling[j, col, p] for j in fr])
                for r in fr:
                    steps[r, col, p] = -v[r]
            for col in fr:
                v = times(steps, p, [maps[direction, j, col] for j in fr])
                for r in fr:
                    maps[direction, r, col] = v[r]
            return c

        lax.fori_loop(0, planes, step, 0)
        each(*map_range(direction), lambda d: map_copy(direction, d).start())

    row_id = lax.broadcasted_iota(jnp.int32, (az, rad), 0)

    def half(h):
        direction = h % 2
        coupling, steps = (upper, low_step) if direction == 0 else (lower, high_step)
        ahead = 2 if direction == 0 else 0
        q, _ = place(direction)

        def local_part(p, c):
            other = times(coupling, p, [fld[j, p + ahead] for j in fr])
            for f in fr:
                v = fld[f, p + 1]
                before = jnp.where(row_id == 0, 0.0, pltpu.roll(v, 1, 0))
                after = jnp.where(row_id == az - 1, 0.0, pltpu.roll(v, az - 1, 0))
                part[f, p] = rhs[f, p] + azl[f, p] * before + azr[f, p] * after - other[f]
            return c

        lax.fori_loop(0, planes, local_part, 0)

        for e in range(1, n_sec):
            slot_copy(h, e, False).wait_recv()
        for f in fr:
            line = jnp.concatenate([slot_in[h, t, pl.ds(f, 1), :] for t in range(n_sec)], axis=1)
            hi, lo = split(put_lane[...] * line)
            dims = (((1,), (1,)), ((), ()))
            iface[f] = (lax.dot_general(put_row[...], hi, dims, preferred_element_type=F32)
                        + lax.dot_general(put_row[...], lo, dims, preferred_element_type=F32))
        for side in range(2):
            halo_copy(h, side).wait_recv()

        def forward(i, y):
            p = i if direction == 0 else planes - 1 - i
            source = []
            for f in fr:
                before = jnp.where(row_id == 0, halo_in[h, 0, f, pl.ds(p, 1), :], 0.0)
                after = jnp.where(row_id == az - 1, halo_in[h, 1, f, pl.ds(p, 1), :], 0.0)
                source.append(part[f, p] + azl[f, p] * before + azr[f, p] * after
                              + iface[f, pl.ds(pl.multiple_of(p * az, az), az), :])
            driven = times(dinv, p, source)
            for f in fr:
                drive[f, p] = driven[f]
            moved = times(steps, p, y)
            return tuple(moved[f] + driven[f] for f in fr)

        zero = tuple(jnp.zeros((az, rad), F32) for _ in fr)
        y = lax.fori_loop(0, planes, forward, zero)
        for f in fr:
            offs[h, f] = y[f]
        each(1, n_ax - q, lambda d: off_copy(h, d).start())
        if h == 0:
            build_map(upper, high_step, 1)
        if h < 2:
            each(1, q, lambda d: map_copy(direction, d).wait_recv())

        entry[...] = jnp.zeros_like(entry)

        @pl.when(q > 0)
        def _():
            off_copy(h, q).wait_recv()
            entry[...] = off_in[h, q]

            def absorb(i, c):
                d = q - i
                off_copy(h, d).wait_recv()
                x = [entry[j] for j in fr]
                for r in fr:
                    entry[r] = sum(map_in[direction, d, r, j] * x[j] for j in fr) + off_in[h, d, r]
                return c

            lax.fori_loop(1, q, absorb, 0)

        for f in fr:
            fld[f, 0 if direction == 0 else planes + 1] = entry[f]

        def replay(i, x):
            p = i if direction == 0 else planes - 1 - i
            moved = times(steps, p, x)
            new = tuple(moved[f] + drive[f, p] for f in fr)
            for f in fr:
                if h == halves - 1:
                    out[f, p] = new[f]
                else:
                    fld[f, p + 1] = new[f]
            return new

        lax.fori_loop(0, planes, replay, tuple(entry[f] for f in fr))

    fld[:, 1:planes + 1] = start[...]
    one_hots(recv_cells, pick_row, pick_lane)
    slot_id = lax.broadcasted_iota(jnp.int32, (1, cap), 1)
    for t in range(n_sec):
        for f in fr:
            live_w[pl.ds(f, 1), t * cap:(t + 1) * cap] = jnp.where(
                slot_id < counts[0, 0, t], weight[0, 0, f, pl.ds(t, 1), :], 0.0)
    for t in range(n_sec):
        for h in range(halves):
            slot_out[h, t] = jnp.zeros_like(slot_out[h, t])
    pl.semaphore_wait(barrier, n_sec - 1 + n_ax - 1)

    @pl.when(a > 0)
    def _():
        edge_copy().start()

    send_field(0)
    build_map(lower, low_step, 0)
    one_hots(donor, put_row, put_lane)

    @pl.when(a < n_ax - 1)
    def _():
        edge_copy().wait_recv()
        fld[:, planes + 1] = edge[...]

    @pl.when(a == n_ax - 1)
    def _():
        fld[:, planes + 1] = jnp.zeros_like(edge)

    for h in range(halves):
        if h:
            send_field(h)
        half(h)

    @pl.when(a > 0)
    def _():
        edge_copy().wait_send()

    for direction in range(2):
        each(*map_range(direction), lambda d: map_copy(direction, d).wait_send())
    for h in range(halves):
        q, _ = place(h % 2)
        each(1, n_ax - q, lambda d: off_copy(h, d).wait_send())
        for side in range(2):
            halo_copy(h, side).wait_send()
        for e in range(1, n_sec):
            slot_copy(h, e, True).wait_send()


def shards(n_ax, n_sec, *args):
    fields, planes, az, rad = args[0].shape
    cap = args[8].shape[-1]
    rows, slots, halves = planes * az, n_sec * cap, 2 * SWEEPS
    vm, dma = pltpu.VMEM, pltpu.SemaphoreType.DMA
    square, line = (fields, fields), (az, rad)
    vmem = pl.BlockSpec(memory_space=pltpu.VMEM)
    specs = [vmem] * 7 + [pl.BlockSpec(memory_space=pltpu.SMEM)] + [vmem] * 3
    return pl.pallas_call(
        functools.partial(kernel, n_ax, n_sec),
        out_shape=jax.ShapeDtypeStruct(args[0].shape, F32),
        in_specs=specs,
        out_specs=vmem,
        scratch_shapes=[
            vm((fields, planes + 2) + line, F32),
            vm(square + (planes,) + line, F32),
            vm(square + (planes,) + line, F32),
            vm((2,) + square + line, F32),
            vm((2, n_ax) + square + line, F32),
            vm((halves, fields) + line, F32),
            vm((halves, n_ax, fields) + line, F32),
            vm((fields,) + line, F32),
            vm((fields,) + line, F32),
            vm((halves, 2, fields, planes, rad), F32),
            vm((halves, 2, fields, planes, rad), F32),
            vm((halves, n_sec, 8, cap), F32),
            vm((halves, n_sec, 8, cap), F32),
            vm((fields, planes) + line, F32),
            vm((fields, planes) + line, F32),
            vm((rows, slots), BF),
            vm((rad, slots), F32),
            vm((rows, slots), BF),
            vm((rad, slots), F32),
            vm((8, slots), F32),
            vm((fields, rows, rad), F32),
            dma((2, n_ax)), dma((2, n_ax)),
            dma((halves, n_ax)), dma((halves, n_ax)),
            dma((1,)), dma((1,)),
            dma((halves, 2)), dma((halves, 2)),
            dma((halves, n_sec)), dma((halves, n_sec)),
        ],
        compiler_params=pltpu.CompilerParams(
            collective_id=0, has_side_effects=True, vmem_limit_bytes=48 * 1024 * 1024
        ),
    )(*args)


def solution(mesh):
    in_specs = (
        P(None, "axial", "sector", None),
        P(None, "axial", "sector", None),
        P(None, None, "axial", "sector", None),
        P(None, None, "axial", "sector", None),
        P(None, None, "axial", "sector", None),
        P(None, "axial", "sector", None),
        P(None, "axial", "sector", None),
        P("axial", "sector", None),
        P("axial", "sector", None, None),
        P("axial", "sector", None, None),
        P("axial", "sector", None, None, None),
    )
    body = functools.partial(shards, mesh.shape["axial"], mesh.shape["sector"])
    return jax.shard_map(body, mesh=mesh, in_specs=in_specs,
                         out_specs=P(None, "axial", "sector", None), check_vma=False)
```

time: 689 us -> 77.4 us (0.11); the launches traced: 676 us -> 77 us
  other arithmetic: 289 us -> 0 us
  blocking collectives: 262 us -> 0 us
  local copies, waits for them, and re-layouts: 90.6 us -> 10.2 us
  Pallas kernels: 0 us -> 66.8 us
  starting transfers between devices: 28.4 us -> 0 us
    all_gather x8 -> x0, blocking collectives: 262 us -> none  [the longest x4 136 us: carry_in(): lax.all_gather(span_map[None], 'axial', axis=0, tiled=True)]
    reduce_sum x233 -> x0, other arithmetic: 143 us -> none  [the longest x168 136 us: apply_block(): return jnp.sum(matrix * vector[None], axis=1)]
    pallas_call x0 -> x1, Pallas kernels: none -> 66.8 us  [shards(): pl.pallas_call(functools.partial(kernel, n_ax, n_sec), out_shape=jax.Shap...]
    add x128 -> x0, other arithmetic: 47.9 us -> none  [the longest x64 24.1 us: compose_step(): apply_block(matrix, carried[1]) + pushed]
    dynamic_update_slice x64 -> x0, other arithmetic: 43.5 us -> none  [replay(): lax.dynamic_update_index_in_dim(carried[1], updated, plane_id, 1)]
    reshape x8 -> x0, local copies, waits for them, and re-layouts: 26.5 us -> none  [the longest x4 23.8 us: sliding_boundary_contribution(): return gathered_sum.reshape(field_now.shape)]
    scatter-add x4 -> x0, other arithmetic: 25.1 us -> none  [sliding_boundary_contribution(): gathered_sum = jnp.zeros((fields, cell_count), jnp.float32).at[:, donor_r...]
    gather x8 -> x0, local copies, waits for them, and re-layouts: 21.8 us -> none  [sliding_boundary_contribution(): picked = flattened[:, receivers]]
  transfers between devices with their start and end apart: 16 -> 0, of which waited for: 0 -> 0; matrix products, arithmetic and copies ran while one was open for 13% -> 0% of each run, Pallas kernels for 0% -> 0%
where the time goes in v1:
time: 77.4 us; the launch traced here: 77 us
  Pallas kernels  66.8 us (86%)
  local copies, waits for them, and re-layouts  10.2 us (13%)
    pallas_call x1, Pallas kernels, shards(): pl.pallas_call(functools.partial(kernel, n_ax, n_sec), out_shape=jax.Shap...  66.8 us
    unnamed x21, local copies, waits for them, and re-layouts  10.2 us

profile of v1, /device:TPU:0, one launch (start us, length us, event | category | flops | bytes accessed | tf_op | source)
XLA Modules:
  0.0 77.0 jit_solution(13407704066427555026)
XLA Ops:
  0.0 0.0 copy-start
  0.0 1.4 %copy-done = f32[5,5,16,8,128]{4,3,2,1,0:T(8,128)S(1)} copy-done((f32[5,5,16,8,128]{4,3,2,1,0:T(8,128)S(1)}, f32[5,5,16,8,128]{4,3,2,1,0:T(8,128)}, u32[]{:S(2)}) %copy-start) | copy-done | bytes 1638424
  1.4 0.0 copy-start.1
  1.4 1.4 %copy-done.1 = f32[5,5,16,8,128]{4,3,2,1,0:T(8,128)S(1)} copy-done((f32[5,5,16,8,128]{4,3,2,1,0:T(8,128)S(1)}, f32[5,5,16,8,128]{4,3,2,1,0:T(8,128)}, u32[]{:S(2)}) %copy-start.1) | copy-done | bytes 1638424
  2.9 0.0 copy-start.2
  2.9 1.0 %copy-done.2 = f32[5,16,8,128]{3,2,1,0:T(8,128)S(1)} copy-done((f32[5,16,8,128]{3,2,1,0:T(8,128)S(1)}, f32[5,16,8,128]{3,2,1,0:T(8,128)}, u32[]{:S(2)}) %copy-start.2) | copy-done | bytes 327704
  3.8 0.0 copy-start.3
  3.8 1.0 %copy-done.3 = f32[5,16,8,128]{3,2,1,0:T(8,128)S(1)} copy-done((f32[5,16,8,128]{3,2,1,0:T(8,128)S(1)}, f32[5,16,8,128]{3,2,1,0:T(8,128)}, u32[]{:S(2)}) %copy-start.3) | copy-done | bytes 327704
  4.8 0.0 copy-start.4
  4.8 1.0 %copy-done.4 = f32[5,16,8,128]{3,2,1,0:T(8,128)S(1)} copy-done((f32[5,16,8,128]{3,2,1,0:T(8,128)S(1)}, f32[5,16,8,128]{3,2,1,0:T(8,128)}, u32[]{:S(2)}) %copy-start.4) | copy-done | bytes 327704
  5.8 0.0 copy-start.5
  5.8 1.0 %copy-done.5 = f32[5,16,8,128]{3,2,1,0:T(8,128)S(1)} copy-done((f32[5,16,8,128]{3,2,1,0:T(8,128)S(1)}, f32[5,16,8,128]{3,2,1,0:T(8,128)}, u32[]{:S(2)}) %copy-start.5) | copy-done | bytes 327704
  6.8 0.0 copy-start.6
  6.8 0.7 copy-done.6
  7.5 0.0 copy-start.7
  7.5 0.7 copy-done.7
  8.1 0.0 copy-start.8
  8.1 0.7 copy-done.8
  8.8 0.0 copy-start.9
  8.8 0.7 copy-done.9
  9.5 66.8 %shard_map.109 = f32[5,16,8,128]{3,2,1,0:T(8,128)S(1)} custom-call(f32[5,16,8,128]{3,2,1,0:T(8,128)S(1)} %copy-done.2, f32[5,16,8,128]{3,2,1,0:T(8,128)S(1)} %copy-done.3, f32[5,5,16,8,128]{4,3,2,1,0:T(8,128)S(1)} %copy-done, f32[5,5,16,8,128]{4,3,2,1,0:T(8,128)S(1)} %copy-done.1, f32[5,5,16,8,128]{4,3,2,1,0:T(8,128)} %upper.1, ...), custom_call_target="tpu_custom_call" | custom-call | tf_op jit(solution)/shard_map/pallas_call | solution.py:272
  76.3 0.7 copy.13
Async XLA Ops:
  0.0 1.4 %copy-start = (f32[5,5,16,8,128]{4,3,2,1,0:T(8,128)S(1)}, f32[5,5,16,8,128]{4,3,2,1,0:T(8,128)}, u32[]{:S(2)}) copy-start(f32[5,5,16,8,128]{4,3,2,1,0:T(8,128)} %dinv.1) | copy-start | bytes 4915204
  1.4 1.4 %copy-start.1 = (f32[5,5,16,8,128]{4,3,2,1,0:T(8,128)S(1)}, f32[5,5,16,8,128]{4,3,2,1,0:T(8,128)}, u32[]{:S(2)}) copy-start(f32[5,5,16,8,128]{4,3,2,1,0:T(8,128)} %lower.1) | copy-start | bytes 4915204
  2.9 1.0 %copy-start.2 = (f32[5,16,8,128]{3,2,1,0:T(8,128)S(1)}, f32[5,16,8,128]{3,2,1,0:T(8,128)}, u32[]{:S(2)}) copy-start(f32[5,16,8,128]{3,2,1,0:T(8,128)} %start.1) | copy-start | bytes 983044
  3.8 1.0 %copy-start.3 = (f32[5,16,8,128]{3,2,1,0:T(8,128)S(1)}, f32[5,16,8,128]{3,2,1,0:T(8,128)}, u32[]{:S(2)}) copy-start(f32[5,16,8,128]{3,2,1,0:T(8,128)} %rhs.1) | copy-start | bytes 983044
  4.8 1.0 %copy-start.4 = (f32[5,16,8,128]{3,2,1,0:T(8,128)S(1)}, f32[5,16,8,128]{3,2,1,0:T(8,128)}, u32[]{:S(2)}) copy-start(f32[5,16,8,128]{3,2,1,0:T(8,128)} %azl.1) | copy-start | bytes 983044
  5.8 1.0 %copy-start.5 = (f32[5,16,8,128]{3,2,1,0:T(8,128)S(1)}, f32[5,16,8,128]{3,2,1,0:T(8,128)}, u32[]{:S(2)}) copy-start(f32[5,16,8,128]{3,2,1,0:T(8,128)} %azr.1) | copy-start | bytes 983044
  6.8 0.7 copy-start.6
  7.5 0.7 copy-start.7
  8.1 0.7 copy-start.8
  8.8 0.7 copy-start.9

commit v2 on v1

--- a/solution.py
+++ b/solution.py
@@ -18,10 +18,18 @@
     return hi, (x - hi.astype(F32)).astype(BF)
 
 
-def kernel(n_ax, n_sec, start, rhs, dinv, lower, upper, azl, azr, counts, recv_cells, donor, weight, out,
-           fld, low_step, high_step, maps, map_in, offs, off_in, entry, edge, halo_out, halo_in,
-           slot_out, slot_in, part, drive, pick_row, pick_lane, put_row, put_lane, live_w, iface,
-           map_ss, map_rs, off_ss, off_rs, edge_ss, edge_rs, halo_ss, halo_rs, slot_ss, slot_rs):
+def dot5(left, right):
+    terms = [x * y for x, y in zip(left, right)]
+    while len(terms) > 1:
+        terms = [sum(terms[i + 1:i + 2], terms[i]) for i in range(0, len(terms), 2)]
+    return terms[0]
+
+
+def kernel(n_ax, n_sec, *refs):
+    (start_h, rhs_h, dinv_h, lower_h, upper_h, azl_h, azr_h, counts, cells_h, donor_h, weight_h, out,
+     start, rhs, dinv, lower, upper, azl, azr, recv_cells, donor, weight, in_sem, fld, low_step, high_step, maps, mate_map, late_map, pair_map, map_in, offs, mate_off, pair_off, off_in, entry,
+     edge, halo_out, halo_in, slot_out, slot_in, part, drive, pick_row, pick_lane, put_row, put_lane, live_w, iface,
+     mate_ss, mate_rs, map_ss, map_rs, off_ss, off_rs, edge_ss, edge_rs, halo_ss, halo_rs, slot_ss, slot_rs) = refs
     fields, planes, az, rad = rhs.shape
     cap = recv_cells.shape[-1]
     rows = planes * az
@@ -30,32 +38,52 @@
     right, left = lax.rem(s + 1, n_sec), lax.rem(s + n_sec - 1, n_sec)
     halves = 2 * SWEEPS
 
+    loads = [pltpu.make_async_copy(src, dst, in_sem.at[i]) for i, (src, dst) in enumerate([
+        (start_h, start), (cells_h, recv_cells), (weight_h, weight), (dinv_h, dinv), (lower_h, lower),
+        (upper_h, upper), (rhs_h, rhs), (azl_h, azl), (azr_h, azr), (donor_h, donor)])]
+    for load in loads:
+        load.start()
+
     barrier = pltpu.get_barrier_semaphore()
     for e in range(1, n_sec):
         pl.semaphore_signal(barrier, inc=1, device_id={"sector": lax.rem(s + e, n_sec)}, device_id_type=MESH)
     for d in range(1, n_ax):
         pl.semaphore_signal(barrier, inc=1, device_id={"axial": lax.rem(a + d, n_ax)}, device_id_type=MESH)
 
+    n_pair = n_ax // 2
+
     def place(direction):
-        return (a, 1) if direction == 0 else (n_ax - 1 - a, -1)
+        q = a if direction == 0 else n_ax - 1 - a
+        return q // 2, lax.rem(q, 2)
 
     def remote(src, dst, ss, rs, **device):
         return pltpu.make_async_remote_copy(src_ref=src, dst_ref=dst, send_sem=ss, recv_sem=rs,
                                             device_id=device, device_id_type=MESH)
 
+    mate = a + 1 - 2 * lax.rem(a, 2)
+
     def peer(direction, d):
-        return lax.rem(a + place(direction)[1] * d + n_ax, n_ax)
+        return lax.rem(a + (2 * d if direction == 0 else 2 * (n_ax - d)), n_ax)
+
+    def mate_copy(src, dst, k):
+        return remote(src, dst, mate_ss.at[k], mate_rs.at[k], axial=mate)
+
+    def mate_map_copy(direction):
+        return mate_copy(maps.at[direction], mate_map.at[direction], 2 * SWEEPS + direction)
+
+    def mate_off_copy(h):
+        return mate_copy(offs.at[h], mate_off.at[h], h)
 
     def map_copy(direction, d):
-        return remote(maps.at[direction], map_in.at[direction, d], map_ss.at[direction, d],
+        return remote(pair_map.at[direction], map_in.at[direction, d], map_ss.at[direction, d],
                       map_rs.at[direction, d], axial=peer(direction, d))
 
     def off_copy(h, d):
-        return remote(offs.at[h], off_in.at[h, d], off_ss.at[h, d], off_rs.at[h, d], axial=peer(h % 2, d))
+        return remote(pair_off.at[h], off_in.at[h, d], off_ss.at[h, d], off_rs.at[h, d], axial=peer(h % 2, d))
 
     def map_range(direction):
-        q, _ = place(direction)
-        return 1, jnp.where(q >= 1, n_ax - q, 1)
+        z, _ = place(direction)
+        return 1, jnp.where(z >= 1, n_pair - z, 1)
 
     def edge_copy():
         return remote(start.at[:, 0], edge, edge_ss.at[0], edge_rs.at[0], axial=lax.rem(a + n_ax - 1, n_ax))
@@ -86,7 +114,7 @@
             lane_ref[:, cols] = jnp.where(across == lax.rem(idx, rad), 1.0, 0.0)
 
     def times(mat, p, x):
-        return [sum(mat[i, j, p] * x[j] for j in fr) for i in fr]
+        return [dot5([mat[i, j, p] for j in fr], x) for i in fr]
 
     def send_field(h):
         for side, layer in ((0, az - 1), (1, 0)):
@@ -122,7 +150,19 @@
                     maps[direction, r, col] = v[r]
             return c
 
-        lax.fori_loop(0, planes, step, 0)
+        lax.fori_loop(0, planes, step, 0, unroll=4)
+        mate_map_copy(direction).start()
+
+    def pair_up(direction):
+        _, late = place(direction)
+        mate_map_copy(direction).wait_recv()
+        for r in fr:
+            for j in fr:
+                late_map[direction, r, j] = jnp.where(late == 1, maps[direction, r, j], mate_map[direction, r, j])
+        for col in fr:
+            first = [jnp.where(late == 1, mate_map[direction, j, col], maps[direction, j, col]) for j in fr]
+            for r in fr:
+                pair_map[direction, r, col] = dot5([late_map[direction, r, j] for j in fr], first)
         each(*map_range(direction), lambda d: map_copy(direction, d).start())
 
     row_id = lax.broadcasted_iota(jnp.int32, (az, rad), 0)
@@ -131,7 +171,7 @@
         direction = h % 2
         coupling, steps = (upper, low_step) if direction == 0 else (lower, high_step)
         ahead = 2 if direction == 0 else 0
-        q, _ = place(direction)
+        z, late = place(direction)
 
         def local_part(p, c):
             other = times(coupling, p, [fld[j, p + ahead] for j in fr])
@@ -142,7 +182,9 @@
                 part[f, p] = rhs[f, p] + azl[f, p] * before + azr[f, p] * after - other[f]
             return c
 
-        lax.fori_loop(0, planes, local_part, 0)
+        lax.fori_loop(0, planes, local_part, 0, unroll=16)
+        if h == 1:
+            pair_up(1)
 
         for e in range(1, n_sec):
             slot_copy(h, e, False).wait_recv()
@@ -170,31 +212,45 @@
             return tuple(moved[f] + driven[f] for f in fr)
 
         zero = tuple(jnp.zeros((az, rad), F32) for _ in fr)
-        y = lax.fori_loop(0, planes, forward, zero)
+        y = lax.fori_loop(0, planes, forward, zero, unroll=16)
         for f in fr:
             offs[h, f] = y[f]
-        each(1, n_ax - q, lambda d: off_copy(h, d).start())
+        mate_off_copy(h).start()
+        if h == 0:
+            pair_up(0)
+        mate_off_copy(h).wait_recv()
+        first = [jnp.where(late == 1, mate_off[h, j], y[j]) for j in fr]
+        for r in fr:
+            last = jnp.where(late == 1, y[r], mate_off[h, r])
+            pair_off[h, r] = dot5([late_map[direction, r, j] for j in fr], first) + last
+        each(1, n_pair - z, lambda d: off_copy(h, d).start())
         if h == 0:
             build_map(upper, high_step, 1)
         if h < 2:
-            each(1, q, lambda d: map_copy(direction, d).wait_recv())
+            each(1, z, lambda d: map_copy(direction, d).wait_recv())
 
         entry[...] = jnp.zeros_like(entry)
 
-        @pl.when(q > 0)
+        @pl.when(z > 0)
         def _():
-            off_copy(h, q).wait_recv()
-            entry[...] = off_in[h, q]
+            off_copy(h, z).wait_recv()
+            entry[...] = off_in[h, z]
 
             def absorb(i, c):
-                d = q - i
+                d = z - i
                 off_copy(h, d).wait_recv()
                 x = [entry[j] for j in fr]
                 for r in fr:
-                    entry[r] = sum(map_in[direction, d, r, j] * x[j] for j in fr) + off_in[h, d, r]
+                    entry[r] = dot5([map_in[direction, d, r, j] for j in fr], x) + off_in[h, d, r]
                 return c
 
-            lax.fori_loop(1, q, absorb, 0)
+            lax.fori_loop(1, z, absorb, 0)
+
+        @pl.when(late == 1)
+        def _():
+            x = [entry[j] for j in fr]
+            for r in fr:
+                entry[r] = dot5([mate_map[direction, r, j] for j in fr], x) + mate_off[h, r]
 
         for f in fr:
             fld[f, 0 if direction == 0 else planes + 1] = entry[f]
@@ -210,8 +266,10 @@
                     fld[f, p + 1] = new[f]
             return new
 
-        lax.fori_loop(0, planes, replay, tuple(entry[f] for f in fr))
-
+        lax.fori_loop(0, planes, replay, tuple(entry[f] for f in fr), unroll=16)
+
+    for load in loads[:3]:
+        load.wait()
     fld[:, 1:planes + 1] = start[...]
     one_hots(recv_cells, pick_row, pick_lane)
     slot_id = lax.broadcasted_iota(jnp.int32, (1, cap), 1)
@@ -229,6 +287,8 @@
         edge_copy().start()
 
     send_field(0)
+    for load in loads[3:]:
+        load.wait()
     build_map(lower, low_step, 0)
     one_hots(donor, put_row, put_lane)
 
@@ -251,10 +311,12 @@
         edge_copy().wait_send()
 
     for direction in range(2):
+        mate_map_copy(direction).wait_send()
         each(*map_range(direction), lambda d: map_copy(direction, d).wait_send())
     for h in range(halves):
-        q, _ = place(h % 2)
-        each(1, n_ax - q, lambda d: off_copy(h, d).wait_send())
+        z, _ = place(h % 2)
+        mate_off_copy(h).wait_send()
+        each(1, n_pair - z, lambda d: off_copy(h, d).wait_send())
         for side in range(2):
             halo_copy(h, side).wait_send()
         for e in range(1, n_sec):
@@ -268,20 +330,27 @@
     vm, dma = pltpu.VMEM, pltpu.SemaphoreType.DMA
     square, line = (fields, fields), (az, rad)
     vmem = pl.BlockSpec(memory_space=pltpu.VMEM)
-    specs = [vmem] * 7 + [pl.BlockSpec(memory_space=pltpu.SMEM)] + [vmem] * 3
+    hbm = pl.BlockSpec(memory_space=pltpu.HBM)
+    specs = [hbm] * 7 + [pl.BlockSpec(memory_space=pltpu.SMEM)] + [hbm] * 3
     return pl.pallas_call(
         functools.partial(kernel, n_ax, n_sec),
         out_shape=jax.ShapeDtypeStruct(args[0].shape, F32),
         in_specs=specs,
         out_specs=vmem,
-        scratch_shapes=[
+        scratch_shapes=[vm(x.shape, x.dtype) for x in args[:7] + args[8:]] + [
+            dma((10,)),
             vm((fields, planes + 2) + line, F32),
             vm(square + (planes,) + line, F32),
             vm(square + (planes,) + line, F32),
             vm((2,) + square + line, F32),
-            vm((2, n_ax) + square + line, F32),
+            vm((2,) + square + line, F32),
+            vm((2,) + square + line, F32),
+            vm((2,) + square + line, F32),
+            vm((2, n_ax // 2) + square + line, F32),
             vm((halves, fields) + line, F32),
-            vm((halves, n_ax, fields) + line, F32),
+            vm((halves, fields) + line, F32),
+            vm((halves, fields) + line, F32),
+            vm((halves, n_ax // 2, fields) + line, F32),
             vm((fields,) + line, F32),
             vm((fields,) + line, F32),
             vm((halves, 2, fields, planes, rad), F32),
@@ -296,8 +365,9 @@
             vm((rad, slots), F32),
             vm((8, slots), F32),
             vm((fields, rows, rad), F32),
-            dma((2, n_ax)), dma((2, n_ax)),
-            dma((halves, n_ax)), dma((halves, n_ax)),
+            dma((halves + 2,)), dma((halves + 2,)),
+            dma((2, n_ax // 2)), dma((2, n_ax // 2)),
+            dma((halves, n_ax // 2)), dma((halves, n_ax // 2)),
             dma((1,)), dma((1,)),
             dma((halves, 2)), dma((halves, 2)),
             dma((halves, n_sec)), dma((halves, n_sec)),

time: 77.4 us -> 65.5 us (0.85)
  Pallas kernels: 66.8 us -> 54.9 us
    pallas_call x1, Pallas kernels: 66.8 us -> 54.9 us  [shards(): pl.pallas_call(functools.partial(kernel, n_ax, n_sec), out_shape=jax.Shap...]
where the time goes in v2:
time: 65.5 us; the launch traced here: 65.1 us
  Pallas kernels  54.9 us (84%)
  local copies, waits for them, and re-layouts  10.2 us (16%)
    pallas_call x1, Pallas kernels, shards(): pl.pallas_call(functools.partial(kernel, n_ax, n_sec), out_shape=jax.Shap...  54.9 us
    unnamed x21, local copies, waits for them, and re-layouts  10.2 us

profile of v2, /device:TPU:0, one launch (start us, length us, event | category | flops | bytes accessed | tf_op | source)
XLA Modules:
  0.0 65.1 jit_solution(6591682382798618136)
XLA Ops:
  0.0 0.0 copy-start
  0.0 1.4 %copy-done = f32[5,5,16,8,128]{4,3,2,1,0:T(8,128)S(1)} copy-done((f32[5,5,16,8,128]{4,3,2,1,0:T(8,128)S(1)}, f32[5,5,16,8,128]{4,3,2,1,0:T(8,128)}, u32[]{:S(2)}) %copy-start) | copy-done | bytes 1638424
  1.4 0.0 copy-start.1
  1.4 1.4 %copy-done.1 = f32[5,5,16,8,128]{4,3,2,1,0:T(8,128)S(1)} copy-done((f32[5,5,16,8,128]{4,3,2,1,0:T(8,128)S(1)}, f32[5,5,16,8,128]{4,3,2,1,0:T(8,128)}, u32[]{:S(2)}) %copy-start.1) | copy-done | bytes 1638424
  2.9 0.0 copy-start.2
  2.9 1.0 %copy-done.2 = f32[5,16,8,128]{3,2,1,0:T(8,128)S(1)} copy-done((f32[5,16,8,128]{3,2,1,0:T(8,128)S(1)}, f32[5,16,8,128]{3,2,1,0:T(8,128)}, u32[]{:S(2)}) %copy-start.2) | copy-done | bytes 327704
  3.8 0.0 copy-start.3
  3.8 1.0 %copy-done.3 = f32[5,16,8,128]{3,2,1,0:T(8,128)S(1)} copy-done((f32[5,16,8,128]{3,2,1,0:T(8,128)S(1)}, f32[5,16,8,128]{3,2,1,0:T(8,128)}, u32[]{:S(2)}) %copy-start.3) | copy-done | bytes 327704
  4.8 0.0 copy-start.4
  4.8 1.0 %copy-done.4 = f32[5,16,8,128]{3,2,1,0:T(8,128)S(1)} copy-done((f32[5,16,8,128]{3,2,1,0:T(8,128)S(1)}, f32[5,16,8,128]{3,2,1,0:T(8,128)}, u32[]{:S(2)}) %copy-start.4) | copy-done | bytes 327704
  5.8 0.0 copy-start.5
  5.8 1.0 %copy-done.5 = f32[5,16,8,128]{3,2,1,0:T(8,128)S(1)} copy-done((f32[5,16,8,128]{3,2,1,0:T(8,128)S(1)}, f32[5,16,8,128]{3,2,1,0:T(8,128)}, u32[]{:S(2)}) %copy-start.5) | copy-done | bytes 327704
  6.8 0.0 copy-start.6
  6.8 0.7 %copy-done.6 = f32[1,1,5,4,128]{4,3,2,1,0:T(4,128)S(1)} copy-done((f32[1,1,5,4,128]{4,3,2,1,0:T(4,128)S(1)}, f32[1,1,5,4,128]{4,3,2,1,0:T(4,128)}, u32[]{:S(2)}) %copy-start.6) | copy-done | bytes 10264
  7.5 0.0 copy-start.7
  7.5 0.7 %copy-done.7 = s32[1,1,4,128]{3,2,1,0:T(4,128)S(1)} copy-done((s32[1,1,4,128]{3,2,1,0:T(4,128)S(1)}, s32[1,1,4,128]{3,2,1,0:T(4,128)}, u32[]{:S(2)}) %copy-start.7) | copy-done | bytes 2072
  8.1 0.0 copy-start.8
  8.1 0.7 %copy-done.8 = s32[1,1,4,128]{3,2,1,0:T(4,128)S(1)} copy-done((s32[1,1,4,128]{3,2,1,0:T(4,128)S(1)}, s32[1,1,4,128]{3,2,1,0:T(4,128)}, u32[]{:S(2)}) %copy-start.8) | copy-done | bytes 2072
  8.8 0.0 copy-start.9
  8.8 0.7 %copy-done.9 = s32[1,1,4]{2,1,0:T(1,128)S(1)} copy-done((s32[1,1,4]{2,1,0:T(1,128)S(1)}, s32[1,1,4]{2,1,0:T(1,128)}, u32[]{:S(2)}) %copy-start.9) | copy-done | bytes 40
  9.5 54.9 %shard_map.109 = f32[5,16,8,128]{3,2,1,0:T(8,128)S(1)} custom-call(f32[5,16,8,128]{3,2,1,0:T(8,128)S(1)} %copy-done.2, f32[5,16,8,128]{3,2,1,0:T(8,128)S(1)} %copy-done.3, f32[5,5,16,8,128]{4,3,2,1,0:T(8,128)S(1)} %copy-done, f32[5,5,16,8,128]{4,3,2,1,0:T(8,128)S(1)} %copy-done.1, f32[5,5,16,8,128]{4,3,2,1,0:T(8,128)} %refs_4_.1, ...), custom_call_target="tpu_custom_call" | custom-call | tf_op jit(solution)/shard_map/pallas_call | solution.py:335
  64.4 0.7 %copy.13 = f32[5,16,8,128]{3,2,1,0:T(8,128)} copy(f32[5,16,8,128]{3,2,1,0:T(8,128)S(1)} %shard_map.109) | data formatting | bytes 655360
Async XLA Ops:
  0.0 1.4 %copy-start = (f32[5,5,16,8,128]{4,3,2,1,0:T(8,128)S(1)}, f32[5,5,16,8,128]{4,3,2,1,0:T(8,128)}, u32[]{:S(2)}) copy-start(f32[5,5,16,8,128]{4,3,2,1,0:T(8,128)} %refs_2_.1) | copy-start | bytes 4915204
  1.4 1.4 %copy-start.1 = (f32[5,5,16,8,128]{4,3,2,1,0:T(8,128)S(1)}, f32[5,5,16,8,128]{4,3,2,1,0:T(8,128)}, u32[]{:S(2)}) copy-start(f32[5,5,16,8,128]{4,3,2,1,0:T(8,128)} %refs_3_.1) | copy-start | bytes 4915204
  2.9 1.0 %copy-start.2 = (f32[5,16,8,128]{3,2,1,0:T(8,128)S(1)}, f32[5,16,8,128]{3,2,1,0:T(8,128)}, u32[]{:S(2)}) copy-start(f32[5,16,8,128]{3,2,1,0:T(8,128)} %refs_0_.1) | copy-start | bytes 983044
  3.8 1.0 %copy-start.3 = (f32[5,16,8,128]{3,2,1,0:T(8,128)S(1)}, f32[5,16,8,128]{3,2,1,0:T(8,128)}, u32[]{:S(2)}) copy-start(f32[5,16,8,128]{3,2,1,0:T(8,128)} %refs_1_.1) | copy-start | bytes 983044
  4.8 1.0 %copy-start.4 = (f32[5,16,8,128]{3,2,1,0:T(8,128)S(1)}, f32[5,16,8,128]{3,2,1,0:T(8,128)}, u32[]{:S(2)}) copy-start(f32[5,16,8,128]{3,2,1,0:T(8,128)} %refs_5_.1) | copy-start | bytes 983044
  5.8 1.0 %copy-start.5 = (f32[5,16,8,128]{3,2,1,0:T(8,128)S(1)}, f32[5,16,8,128]{3,2,1,0:T(8,128)}, u32[]{:S(2)}) copy-start(f32[5,16,8,128]{3,2,1,0:T(8,128)} %refs_6_.1) | copy-start | bytes 983044
  6.8 0.7 %copy-start.6 = (f32[1,1,5,4,128]{4,3,2,1,0:T(4,128)S(1)}, f32[1,1,5,4,128]{4,3,2,1,0:T(4,128)}, u32[]{:S(2)}) copy-start(f32[1,1,5,4,128]{4,3,2,1,0:T(4,128)} %refs_10_.1) | copy-start | bytes 30724
  7.5 0.7 %copy-start.7 = (s32[1,1,4,128]{3,2,1,0:T(4,128)S(1)}, s32[1,1,4,128]{3,2,1,0:T(4,128)}, u32[]{:S(2)}) copy-start(s32[1,1,4,128]{3,2,1,0:T(4,128)} %refs_8_.1) | copy-start | bytes 6148
  8.1 0.7 %copy-start.8 = (s32[1,1,4,128]{3,2,1,0:T(4,128)S(1)}, s32[1,1,4,128]{3,2,1,0:T(4,128)}, u32[]{:S(2)}) copy-start(s32[1,1,4,128]{3,2,1,0:T(4,128)} %refs_9_.1) | copy-start | bytes 6148
  8.8 0.7 %copy-start.9 = (s32[1,1,4]{2,1,0:T(1,128)S(1)}, s32[1,1,4]{2,1,0:T(1,128)}, u32[]{:S(2)}) copy-start(s32[1,1,4]{2,1,0:T(1,128)} %refs_7_.1) | copy-start | bytes 52

commit v3 on v2

--- a/solution.py
+++ b/solution.py
@@ -151,7 +151,6 @@
             return c
 
         lax.fori_loop(0, planes, step, 0, unroll=4)
-        mate_map_copy(direction).start()
 
     def pair_up(direction):
         _, late = place(direction)
@@ -224,8 +223,6 @@
             last = jnp.where(late == 1, y[r], mate_off[h, r])
             pair_off[h, r] = dot5([late_map[direction, r, j] for j in fr], first) + last
         each(1, n_pair - z, lambda d: off_copy(h, d).start())
-        if h == 0:
-            build_map(upper, high_step, 1)
         if h < 2:
             each(1, z, lambda d: map_copy(direction, d).wait_recv())
 
@@ -280,16 +277,19 @@
     for t in range(n_sec):
         for h in range(halves):
             slot_out[h, t] = jnp.zeros_like(slot_out[h, t])
+    for load in loads[3:]:
+        load.wait()
+    build_map(lower, low_step, 0)
     pl.semaphore_wait(barrier, n_sec - 1 + n_ax - 1)
 
     @pl.when(a > 0)
     def _():
         edge_copy().start()
 
+    mate_map_copy(0).start()
     send_field(0)
-    for load in loads[3:]:
-        load.wait()
-    build_map(lower, low_step, 0)
+    build_map(upper, high_step, 1)
+    mate_map_copy(1).start()
     one_hots(donor, put_row, put_lane)
 
     @pl.when(a < n_ax - 1)

time: 65.5 us -> 64.9 us (level)
  Pallas kernels: 54.9 us -> 54.2 us
    pallas_call x1, Pallas kernels: 54.9 us -> 54.2 us  [shards(): pl.pallas_call(functools.partial(kernel, n_ax, n_sec), out_shape=jax.Shap...]
where the time goes in v3:
time: 64.9 us; the launch traced here: 64.5 us
  Pallas kernels  54.2 us (84%)
  local copies, waits for them, and re-layouts  10.2 us (16%)
    pallas_call x1, Pallas kernels, shards(): pl.pallas_call(functools.partial(kernel, n_ax, n_sec), out_shape=jax.Shap...  54.2 us
    unnamed x21, local copies, waits for them, and re-layouts  10.2 us

profile of v3, /device:TPU:0, one launch (start us, length us, event | category | flops | bytes accessed | tf_op | source)
XLA Modules:
  0.0 64.5 jit_solution(10170741615009167998)
XLA Ops:
  0.0 0.0 copy-start
  0.0 1.4 %copy-done = f32[5,5,16,8,128]{4,3,2,1,0:T(8,128)S(1)} copy-done((f32[5,5,16,8,128]{4,3,2,1,0:T(8,128)S(1)}, f32[5,5,16,8,128]{4,3,2,1,0:T(8,128)}, u32[]{:S(2)}) %copy-start) | copy-done | bytes 1638424
  1.4 0.0 copy-start.1
  1.4 1.4 %copy-done.1 = f32[5,5,16,8,128]{4,3,2,1,0:T(8,128)S(1)} copy-done((f32[5,5,16,8,128]{4,3,2,1,0:T(8,128)S(1)}, f32[5,5,16,8,128]{4,3,2,1,0:T(8,128)}, u32[]{:S(2)}) %copy-start.1) | copy-done | bytes 1638424
  2.9 0.0 copy-start.2
  2.9 1.0 %copy-done.2 = f32[5,16,8,128]{3,2,1,0:T(8,128)S(1)} copy-done((f32[5,16,8,128]{3,2,1,0:T(8,128)S(1)}, f32[5,16,8,128]{3,2,1,0:T(8,128)}, u32[]{:S(2)}) %copy-start.2) | copy-done | bytes 327704
  3.8 0.0 copy-start.3
  3.8 1.0 %copy-done.3 = f32[5,16,8,128]{3,2,1,0:T(8,128)S(1)} copy-done((f32[5,16,8,128]{3,2,1,0:T(8,128)S(1)}, f32[5,16,8,128]{3,2,1,0:T(8,128)}, u32[]{:S(2)}) %copy-start.3) | copy-done | bytes 327704
  4.8 0.0 copy-start.4
  4.8 1.0 %copy-done.4 = f32[5,16,8,128]{3,2,1,0:T(8,128)S(1)} copy-done((f32[5,16,8,128]{3,2,1,0:T(8,128)S(1)}, f32[5,16,8,128]{3,2,1,0:T(8,128)}, u32[]{:S(2)}) %copy-start.4) | copy-done | bytes 327704
  5.8 0.0 copy-start.5
  5.8 1.0 %copy-done.5 = f32[5,16,8,128]{3,2,1,0:T(8,128)S(1)} copy-done((f32[5,16,8,128]{3,2,1,0:T(8,128)S(1)}, f32[5,16,8,128]{3,2,1,0:T(8,128)}, u32[]{:S(2)}) %copy-start.5) | copy-done | bytes 327704
  6.8 0.0 copy-start.6
  6.8 0.7 %copy-done.6 = f32[1,1,5,4,128]{4,3,2,1,0:T(4,128)S(1)} copy-done((f32[1,1,5,4,128]{4,3,2,1,0:T(4,128)S(1)}, f32[1,1,5,4,128]{4,3,2,1,0:T(4,128)}, u32[]{:S(2)}) %copy-start.6) | copy-done | bytes 10264
  7.5 0.0 copy-start.7
  7.5 0.7 %copy-done.7 = s32[1,1,4,128]{3,2,1,0:T(4,128)S(1)} copy-done((s32[1,1,4,128]{3,2,1,0:T(4,128)S(1)}, s32[1,1,4,128]{3,2,1,0:T(4,128)}, u32[]{:S(2)}) %copy-start.7) | copy-done | bytes 2072
  8.1 0.0 copy-start.8
  8.1 0.7 %copy-done.8 = s32[1,1,4,128]{3,2,1,0:T(4,128)S(1)} copy-done((s32[1,1,4,128]{3,2,1,0:T(4,128)S(1)}, s32[1,1,4,128]{3,2,1,0:T(4,128)}, u32[]{:S(2)}) %copy-start.8) | copy-done | bytes 2072
  8.8 0.0 copy-start.9
  8.8 0.7 %copy-done.9 = s32[1,1,4]{2,1,0:T(1,128)S(1)} copy-done((s32[1,1,4]{2,1,0:T(1,128)S(1)}, s32[1,1,4]{2,1,0:T(1,128)}, u32[]{:S(2)}) %copy-start.9) | copy-done | bytes 40
  9.5 54.2 %shard_map.109 = f32[5,16,8,128]{3,2,1,0:T(8,128)S(1)} custom-call(f32[5,16,8,128]{3,2,1,0:T(8,128)S(1)} %copy-done.2, f32[5,16,8,128]{3,2,1,0:T(8,128)S(1)} %copy-done.3, f32[5,5,16,8,128]{4,3,2,1,0:T(8,128)S(1)} %copy-done, f32[5,5,16,8,128]{4,3,2,1,0:T(8,128)S(1)} %copy-done.1, f32[5,5,16,8,128]{4,3,2,1,0:T(8,128)} %refs_4_.1, ...), custom_call_target="tpu_custom_call" | custom-call | tf_op jit(solution)/shard_map/pallas_call | solution.py:335
  63.7 0.7 %copy.13 = f32[5,16,8,128]{3,2,1,0:T(8,128)} copy(f32[5,16,8,128]{3,2,1,0:T(8,128)S(1)} %shard_map.109) | data formatting | bytes 655360
Async XLA Ops:
  0.0 1.4 %copy-start = (f32[5,5,16,8,128]{4,3,2,1,0:T(8,128)S(1)}, f32[5,5,16,8,128]{4,3,2,1,0:T(8,128)}, u32[]{:S(2)}) copy-start(f32[5,5,16,8,128]{4,3,2,1,0:T(8,128)} %refs_2_.1) | copy-start | bytes 4915204
  1.4 1.4 %copy-start.1 = (f32[5,5,16,8,128]{4,3,2,1,0:T(8,128)S(1)}, f32[5,5,16,8,128]{4,3,2,1,0:T(8,128)}, u32[]{:S(2)}) copy-start(f32[5,5,16,8,128]{4,3,2,1,0:T(8,128)} %refs_3_.1) | copy-start | bytes 4915204
  2.9 1.0 %copy-start.2 = (f32[5,16,8,128]{3,2,1,0:T(8,128)S(1)}, f32[5,16,8,128]{3,2,1,0:T(8,128)}, u32[]{:S(2)}) copy-start(f32[5,16,8,128]{3,2,1,0:T(8,128)} %refs_0_.1) | copy-start | bytes 983044
  3.8 1.0 %copy-start.3 = (f32[5,16,8,128]{3,2,1,0:T(8,128)S(1)}, f32[5,16,8,128]{3,2,1,0:T(8,128)}, u32[]{:S(2)}) copy-start(f32[5,16,8,128]{3,2,1,0:T(8,128)} %refs_1_.1) | copy-start | bytes 983044
  4.8 1.0 %copy-start.4 = (f32[5,16,8,128]{3,2,1,0:T(8,128)S(1)}, f32[5,16,8,128]{3,2,1,0:T(8,128)}, u32[]{:S(2)}) copy-start(f32[5,16,8,128]{3,2,1,0:T(8,128)} %refs_5_.1) | copy-start | bytes 983044
  5.8 1.0 %copy-start.5 = (f32[5,16,8,128]{3,2,1,0:T(8,128)S(1)}, f32[5,16,8,128]{3,2,1,0:T(8,128)}, u32[]{:S(2)}) copy-start(f32[5,16,8,128]{3,2,1,0:T(8,128)} %refs_6_.1) | copy-start | bytes 983044
  6.8 0.7 %copy-start.6 = (f32[1,1,5,4,128]{4,3,2,1,0:T(4,128)S(1)}, f32[1,1,5,4,128]{4,3,2,1,0:T(4,128)}, u32[]{:S(2)}) copy-start(f32[1,1,5,4,128]{4,3,2,1,0:T(4,128)} %refs_10_.1) | copy-start | bytes 30724
  7.5 0.7 %copy-start.7 = (s32[1,1,4,128]{3,2,1,0:T(4,128)S(1)}, s32[1,1,4,128]{3,2,1,0:T(4,128)}, u32[]{:S(2)}) copy-start(s32[1,1,4,128]{3,2,1,0:T(4,128)} %refs_8_.1) | copy-start | bytes 6148
  8.1 0.7 %copy-start.8 = (s32[1,1,4,128]{3,2,1,0:T(4,128)S(1)}, s32[1,1,4,128]{3,2,1,0:T(4,128)}, u32[]{:S(2)}) copy-start(s32[1,1,4,128]{3,2,1,0:T(4,128)} %refs_9_.1) | copy-start | bytes 6148
  8.8 0.7 %copy-start.9 = (s32[1,1,4]{2,1,0:T(1,128)S(1)}, s32[1,1,4]{2,1,0:T(1,128)}, u32[]{:S(2)}) copy-start(s32[1,1,4]{2,1,0:T(1,128)} %refs_7_.1) | copy-start | bytes 52
